TPU v7x, 32 devices: a whole 2x2x4 slice. The times are simulated.
32 devices in a mesh: ctx: 8 (over z, y), head: 4 (over x, core).
Axes of the slice: x: 2, y: 2, z: 4, core: 2. Of those that a mesh axis runs over, the one named last changes fastest.
Arguments:
- frozen_queries: bfloat16 [2048, 2048], P('ctx', 'head'), may hold values from -70 to 70
- key_value_rows: bfloat16 [2048, 512], P('ctx'), may hold values from -4.5 to 4.5
- output_gradient: bfloat16 [2048, 2048], P('ctx', 'head'), may hold values from -6 to 6
- inputs: bfloat16 [2048, 8192], P('ctx', 'head'), may hold values from -6 to 6
- adapter_down: float32 [64, 8192], P('ctx', 'head'), may hold values from -0.0625 to 0.0625
- down_first_moment: float32 [64, 8192], P('ctx', 'head'), may hold values from -6 to 6
- down_second_moment: float32 [64, 8192], P('ctx', 'head'), may hold values from 0.5 to 8
- adapter_up: float32 [64, 2048], P('ctx', 'head'), may hold values from -0.75 to 0.75
- up_first_moment: float32 [64, 2048], P('ctx', 'head'), may hold values from -6 to 6
- up_second_moment: float32 [64, 2048], P('ctx', 'head'), may hold values from 0.5 to 8
- rank_keep_mask: int32 [2, 64], replicated, may hold values 0 or 1
- group_length: int32 [2], replicated, may hold values from 256 to 1024, as said below
- group_shift: int32 [2], replicated, may hold values from 1 to 1023
Outputs:
- attention_out: bfloat16 [2048, 2048], P('ctx', 'head')
- query_gradient: bfloat16 [2048, 2048], P('ctx', 'head')
- kv_grad: float32 [2048, 512], P('ctx', 'head')
- updated_down: float32 [64, 8192], P('ctx', 'head')
- updated_down_first: float32 [64, 8192], P('ctx', 'head')
- updated_down_second: float32 [64, 8192], P('ctx', 'head')
- updated_up: float32 [64, 2048], P('ctx', 'head')
- updated_up_first: float32 [64, 2048], P('ctx', 'head')
- updated_up_second: float32 [64, 2048], P('ctx', 'head')
Inputs may be any that keep to these rules, and one draw needn't show every extreme that they name: `group_length`: each key-value head's group holds 1024 rolled positions or fewer, and in every draw some head's group holds exactly 1024.
All inputs are finite; a program needn't handle non-finite values.
Results may differ from a plain program's by a relative error of at most 0.012.
Values may be sent and summed in bfloat16 or wider, within the bound.
A program may use at most 64 MiB of HBM per device.

v0:
```python
import math

import jax
import jax.numpy as jnp
from jax import lax
from jax.sharding import PartitionSpec as P

LOCAL_HEADS = 16
KVH = 2
HEAD_SIZE = 128


adapter_scale = 0.25
beta_one = 0.9
beta_two = 0.999
learn_rate = 0.01
adam_epsilon = 1e-08


def shifted(value, axis, steps):
    count = lax.axis_size(axis)
    pairs = [(source, (source + steps) % count) for source in range(count)]
    return lax.ppermute(value, axis, pairs)


def adam_update(current, moment_one, moment_two, gradient):
    moment_one_new = beta_one * moment_one + (1.0 - beta_one) * gradient
    moment_two_new = beta_two * moment_two + (1.0 - beta_two) * gradient * gradient
    updated = current - learn_rate * moment_one_new / (jnp.sqrt(moment_two_new) + adam_epsilon)
    return (updated, moment_one_new, moment_two_new)


def spread_pair(key_part, value_part, head_slot, key_width):
    holder = jnp.zeros((key_part.shape[0], 2 * key_width), jnp.float32)
    holder = lax.dynamic_update_slice_in_dim(holder, key_part, head_slot * key_part.shape[1], 1)
    return lax.dynamic_update_slice_in_dim(
        holder, value_part, key_width + head_slot * key_part.shape[1], 1
    )


def on_device(
    frozen_queries,
    key_value_rows,
    output_gradient,
    inputs,
    adapter_down,
    down_first_moment,
    down_second_moment,
    adapter_up,
    up_first_moment,
    up_second_moment,
    rank_keep_mask,
    group_length,
    group_shift,
):
    tokens_here = frozen_queries.shape[0]
    ctx_count = lax.axis_size("ctx")
    ctx_place = lax.axis_index("ctx")
    head_place = lax.axis_index("head")
    reach = min(8, ctx_count // 2)
    heads_here = frozen_queries.shape[1] // HEAD_SIZE
    group_heads = LOCAL_HEADS // KVH
    kv_head = head_place * heads_here // group_heads
    seq_total = tokens_here * ctx_count
    key_width = KVH * HEAD_SIZE
    down_keep_mask = rank_keep_mask[0].astype(jnp.float32)
    down_full, up_full = (
        lax.all_gather(adapter_down.astype(jnp.bfloat16), "ctx", axis=0, tiled=True),
        lax.all_gather(adapter_up.astype(jnp.bfloat16), "ctx", axis=0, tiled=True),
    )
    masked_up_factor = up_full * rank_keep_mask[1][:, None].astype(jnp.bfloat16)
    contract_last = (((1,), (1,)), ((), ()))
    contract_first = (((0,), (0,)), ((), ()))
    projected = lax.psum(
        lax.dot_general(
            inputs, down_full, contract_last, preferred_element_type=jnp.float32
        ).astype(jnp.bfloat16),
        "head",
    ).astype(jnp.float32)
    masked_projection = (projected * down_keep_mask[None, :]).astype(jnp.bfloat16)
    query_values = (
        frozen_queries.astype(jnp.float32)
        + adapter_scale
        * jnp.dot(masked_projection, masked_up_factor, preferred_element_type=jnp.float32)
    ).astype(jnp.bfloat16)
    key_own = lax.dynamic_slice_in_dim(key_value_rows, kv_head * HEAD_SIZE, HEAD_SIZE, 1)
    value_own = lax.dynamic_slice_in_dim(
        key_value_rows, key_width + kv_head * HEAD_SIZE, HEAD_SIZE, 1
    )
    pair_own = jnp.concatenate([key_own, value_own], 1)
    within = jnp.arange(tokens_here, dtype=jnp.int32)
    query_place = ctx_place * tokens_here + within
    offset_here = group_shift[kv_head]
    group_here = group_length[kv_head]
    query_rolled = (query_place - offset_here) % seq_total
    query_group = query_rolled // group_here
    score_scale = 1.0 / math.sqrt(HEAD_SIZE)
    query_heads = query_values.reshape(tokens_here, heads_here, HEAD_SIZE)
    grad_heads = output_gradient.reshape(tokens_here, heads_here, HEAD_SIZE)

    def tile_scores(pair_rows, distance):
        source = (ctx_place - distance + ctx_count) % ctx_count
        key_rolled = (source * tokens_here + within - offset_here) % seq_total
        allowed = (query_group[:, None] == (key_rolled // group_here)[None, :]) & (
            key_rolled[None, :] <= query_rolled[:, None]
        )
        scores = (
            jnp.einsum(
                "qhd,kd->hqk",
                query_heads,
                pair_rows[:, :HEAD_SIZE],
                preferred_element_type=jnp.float32,
            )
            * score_scale
        )
        return jnp.where(allowed[None], scores, -1e30)

    def stats_step(carry, pair_rows, distance):
        running_max, running_total = carry
        scores = tile_scores(pair_rows, distance)
        new_max = jnp.maximum(running_max, jnp.max(scores, -1, keepdims=True))
        running_total = running_total * jnp.exp(running_max - new_max) + jnp.sum(
            jnp.exp(scores - new_max), -1, keepdims=True
        )
        return (new_max, running_total)

    start_max = jnp.full((heads_here, tokens_here, 1), -1e30, jnp.float32)
    start_total = jnp.zeros((heads_here, tokens_here, 1), jnp.float32)
    start_stack = jnp.zeros((reach + 1, tokens_here, 2 * HEAD_SIZE), jnp.bfloat16)

    def first_turn(distance, state):
        held, stack, stats = state
        stack = lax.dynamic_update_index_in_dim(stack, held, distance, 0)
        stats = stats_step(stats, held, distance)
        held = shifted(held, "ctx", 1)
        return (held, stack, stats)

    held, stack, stats = lax.fori_loop(
        0, reach, first_turn, (pair_own, start_stack, (start_max, start_total))
    )
    stack = lax.dynamic_update_index_in_dim(stack, held, reach, 0)
    row_max, total = stats_step(stats, held, reach)

    def weights_of(scores):
        return jnp.exp(scores - row_max) / total

    def out_step(carry, pair_rows, distance):
        out_sum, dot_sum = carry
        weights = weights_of(tile_scores(pair_rows, distance))
        weights_half = weights.astype(jnp.bfloat16)
        out_sum = out_sum + jnp.einsum(
            "hqk,kd->qhd",
            weights_half,
            pair_rows[:, HEAD_SIZE:],
            preferred_element_type=jnp.float32,
        )
        grad_weights = jnp.einsum(
            "qhd,kd->hqk", grad_heads, pair_rows[:, HEAD_SIZE:], preferred_element_type=jnp.float32
        )
        dot_sum = dot_sum + jnp.sum(weights * grad_weights, -1, keepdims=True)
        return (out_sum, dot_sum)

    start_out = (
        jnp.zeros((tokens_here, heads_here, HEAD_SIZE), jnp.float32),
        jnp.zeros((heads_here, tokens_here, 1), jnp.float32),
    )

    def second_kept(distance, inner):
        return out_step(inner, lax.dynamic_index_in_dim(stack, distance, 0, False), distance)

    out_sum, row_dots = lax.fori_loop(0, reach + 1, second_kept, start_out)
    attention_out = out_sum.astype(jnp.bfloat16).reshape(tokens_here, heads_here * HEAD_SIZE)

    def grad_tile(pair_rows, distance):
        weights = weights_of(tile_scores(pair_rows, distance))
        weights_half = weights.astype(jnp.bfloat16)
        grad_weights = jnp.einsum(
            "qhd,kd->hqk", grad_heads, pair_rows[:, HEAD_SIZE:], preferred_element_type=jnp.float32
        )
        grad_scores = (weights * (grad_weights - row_dots)).astype(jnp.bfloat16)
        query_part = jnp.einsum(
            "hqk,kd->qhd", grad_scores, pair_rows[:, :HEAD_SIZE], preferred_element_type=jnp.float32
        )
        key_part = score_scale * jnp.einsum(
            "hqk,qhd->kd", grad_scores, query_heads, preferred_element_type=jnp.float32
        )
        value_part = jnp.einsum(
            "hqk,qhd->kd", weights_half, grad_heads, preferred_element_type=jnp.float32
        )
        return (query_part, jnp.concatenate([key_part, value_part], 1))

    start_query = jnp.zeros((tokens_here, heads_here, HEAD_SIZE), jnp.float32)
    start_pair = jnp.zeros((tokens_here, 2 * HEAD_SIZE), jnp.float32)

    def third_kept(index, state):
        grads_held, query_sum = state
        distance = reach - index
        query_part, pair_part = grad_tile(
            lax.dynamic_index_in_dim(stack, distance, 0, False), distance
        )
        grads_held = shifted((grads_held + pair_part).astype(jnp.bfloat16), "ctx", -1).astype(
            jnp.float32
        )
        return (grads_held, query_sum + query_part)

    grads_held, query_sum = lax.fori_loop(0, reach, third_kept, (start_pair, start_query))
    query_part, pair_part = grad_tile(pair_own, 0)
    query_sum = query_sum + query_part
    pair_total = grads_held + pair_part
    query_gradient = (
        (score_scale * query_sum).astype(jnp.bfloat16).reshape(tokens_here, heads_here * HEAD_SIZE)
    )
    holder = spread_pair(pair_total[:, :HEAD_SIZE], pair_total[:, HEAD_SIZE:], kv_head, key_width)
    kv_grad = lax.psum_scatter(
        holder.astype(jnp.bfloat16), "head", scatter_dimension=1, tiled=True
    ).astype(jnp.float32)
    projection_backward = lax.psum(
        lax.dot_general(
            query_gradient, masked_up_factor, contract_last, preferred_element_type=jnp.float32
        ).astype(jnp.bfloat16),
        "head",
    ).astype(jnp.float32)
    rank_product = (projection_backward * down_keep_mask[None, :] * adapter_scale).astype(
        jnp.bfloat16
    )
    part_down = lax.dot_general(
        rank_product, inputs, contract_first, preferred_element_type=jnp.float32
    )
    partial_up = adapter_scale * lax.dot_general(
        masked_projection, query_gradient, contract_first, preferred_element_type=jnp.float32
    )
    local_rows = adapter_down.shape[0]
    sum_down, sum_up = lax.psum((part_down, partial_up), "ctx")
    down_gradient = lax.dynamic_slice_in_dim(sum_down, ctx_place * local_rows, local_rows, 0)
    up_gradient = lax.dynamic_slice_in_dim(sum_up, ctx_place * local_rows, local_rows, 0)
    keep_rows = lax.dynamic_slice_in_dim(
        rank_keep_mask[1], ctx_place * local_rows, local_rows, 0
    ).astype(jnp.float32)
    up_gradient = keep_rows[:, None] * up_gradient
    updated_down, updated_down_first, updated_down_second = adam_update(
        adapter_down, down_first_moment, down_second_moment, down_gradient
    )
    updated_up, updated_up_first, updated_up_second = adam_update(
        adapter_up, up_first_moment, up_second_moment, up_gradient
    )
    return (
        attention_out,
        query_gradient,
        kv_grad,
        updated_down,
        updated_down_first,
        updated_down_second,
        updated_up,
        updated_up_first,
        updated_up_second,
    )


def solution(mesh):
    placed = (
        P("ctx", "head"),
        P("ctx", None),
        P("ctx", "head"),
        P("ctx", "head"),
        P("ctx", "head"),
        P("ctx", "head"),
        P("ctx", "head"),
        P("ctx", "head"),
        P("ctx", "head"),
        P("ctx", "head"),
        P(),
        P(),
        P(),
    )
    return jax.shard_map(
        on_device,
        mesh=mesh,
        in_specs=placed,
        out_specs=(
            P("ctx", "head"),
            P("ctx", "head"),
            P("ctx", "head"),
            P("ctx", "head"),
            P("ctx", "head"),
            P("ctx", "head"),
            P("ctx", "head"),
            P("ctx", "head"),
            P("ctx", "head"),
        ),
        check_vma=False,
    )
```

profile of v0, /device:TPU:0, one launch (start us, length us, event | category | flops | bytes accessed | tf_op | source)
XLA Modules:
  0.0 324.0 jit_solution(6726015293650904589)
XLA Ops:
  8.9 32.4 %all_gather.7 = bf16[64,512]{1,0:T(8,128)(2,1)S(1)} all-gather(bf16[8,512]{1,0:T(8,128)(2,1)S(1)} %convert_element_type.134), channel_id=1, replica_groups=mesh['ctx'=8,'head'=4] {'ctx'}, dimensions={0}, use_global_device_ids=true | all-gather | bytes 73728 | tf_op jit(solution)/shard_map/all_gather | solution.py:69
  42.0 30.7 %all_gather.6 = bf16[64,2048]{1,0:T(8,128)(2,1)S(1)} all-gather(bf16[8,2048]{1,0:T(8,128)(2,1)S(1)} %convert_element_type.129), channel_id=1, replica_groups=mesh['ctx'=8,'head'=4] {'ctx'}, dimensions={0}, use_global_device_ids=true | all-gather | bytes 294912 | tf_op jit(solution)/shard_map/all_gather | solution.py:68
  73.2 10.3 %psum.28 = bf16[256,64]{0,1:T(8,128)(2,1)S(1)} all-reduce(bf16[256,64]{0,1:T(8,128)(2,1)S(1)} %convolution_convert_fusion.1), channel_id=1, replica_groups=mesh['ctx'=8,'head'=4] {'head'}, use_global_device_ids=true, to_apply=%region_0.1 | all-reduce | flops 16384 | bytes 65536 | tf_op jit(solution)/shard_map/psum | solution.py:74
  95.2 31.5 %while.67 = (s32[]{:T(128)}, bf16[256,256]{1,0:T(8,128)(2,1)S(1)}, bf16[5,256,256]{2,1,0:T(8,128)(2,1)}, f32[4,256,1]{1,0,2:T(4,128)S(1)}, f32[4,256,1]{1,0,2:T(...) while((s32[]{:T(128)}, bf16[256,256]{1,0:T(8,128)(2,1)S(1)}, ...), condition=%wide.region_4.5_spmd.clone.clone.clone, body=%wide.region_1.4_spmd.clone.clone.clone.sunk | while | flops 68632080 | bytes 3666309 | solution.py:138
  95.2 1.6 collective-permute-start
  101.7 1.8 collective-permute-done
  108.5 2.7 collective-permute-done
  116.2 2.7 collective-permute-done
  124.0 2.7 collective-permute-done
  130.6 31.8 %while.68 = (s32[]{:T(128)}, f32[256,4,128]{0,2,1:T(8,128)S(1)}, f32[4,256,1]{1,2,0:T(1,128)S(1)}, bf16[5,256,256]{2,1,0:T(8,128)(2,1)}, s32[]{:T(128)}, /*index...) while((s32[]{:T(128)}, f32[256,4,128]{0,2,1:T(8,128)S(1)}, ...), condition=%wide.region_9.10_spmd.clone.clone.clone, body=%wide.region_7.9_spmd.clone.clone.clone.sunk | while | flops 203632144 | bytes 6390153 | solution.py:171
  168.0 54.1 %while.69 = (s32[]{:T(128)}, f32[256,256]{0,1:T(8,128)S(1)}, f32[256,4,128]{0,2,1:T(8,128)S(1)}, s32[]{:T(128)}, s32[]{:T(128)}, /*index=5*/s32[]{:T(128)}, s32[...) while((s32[]{:T(128)}, f32[256,256]{0,1:T(8,128)S(1)}, ...), condition=%wide.region_11.12_spmd.clone.clone.clone, body=%wide.region_10.11_spmd.clone.clone.clone.sunk | while | flops 338471424 | bytes 9277943 | solution.py:206
  173.7 2.0 collective-permute-start.1
  176.0 2.9 collective-permute-done.1
  185.3 4.7 %collective-permute-start.1 = (bf16[256,256]{0,1:T(8,128)(2,1)}, bf16[256,256]{0,1:T(8,128)(2,1)S(1)}, u32[]{:S(2)}, u32[]{:S(2)}) collective-permute-start(bf16[256,256]{0,1:T(8,128)(2,1)} %fusion.158), channel_id=1, source_target_pairs={{0,28},{4,0},{8,4},{12,8},{16,12},{20,16},{24,20},{28,24},{1,29},{... | collective-permute-start | bytes 393224 | tf_op jit(solution)/shard_map/while/body/eval_jaxpr/ppermute | solution.py:23
  190.3 2.5 collective-permute-done.1
  199.2 5.0 %collective-permute-start.1 = (bf16[256,256]{0,1:T(8,128)(2,1)}, bf16[256,256]{0,1:T(8,128)(2,1)S(1)}, u32[]{:S(2)}, u32[]{:S(2)}) collective-permute-start(bf16[256,256]{0,1:T(8,128)(2,1)} %fusion.158), channel_id=1, source_target_pairs={{0,28},{4,0},{8,4},{12,8},{16,12},{20,16},{24,20},{28,24},{1,29},{... | collective-permute-start | bytes 393224 | tf_op jit(solution)/shard_map/while/body/eval_jaxpr/ppermute | solution.py:23
  204.6 2.5 collective-permute-done.1
  213.5 5.0 %collective-permute-start.1 = (bf16[256,256]{0,1:T(8,128)(2,1)}, bf16[256,256]{0,1:T(8,128)(2,1)S(1)}, u32[]{:S(2)}, u32[]{:S(2)}) collective-permute-start(bf16[256,256]{0,1:T(8,128)(2,1)} %fusion.158), channel_id=1, source_target_pairs={{0,28},{4,0},{8,4},{12,8},{16,12},{20,16},{24,20},{28,24},{1,29},{... | collective-permute-start | bytes 393224 | tf_op jit(solution)/shard_map/while/body/eval_jaxpr/ppermute | solution.py:23
  218.9 2.5 collective-permute-done.1
  226.4 10.4 %psum.29 = bf16[256,64]{0,1:T(8,128)(2,1)S(1)} all-reduce(bf16[256,64]{0,1:T(8,128)(2,1)S(1)} %convolution_convert_fusion), channel_id=1, replica_groups=mesh['ctx'=8,'head'=4] {'head'}, use_global_device_ids=true, to_apply=%region_13.14 | all-reduce | flops 16384 | bytes 65536 | tf_op jit(solution)/shard_map/psum | solution.py:217
  241.3 4.6 %reduce-scatter.4.cloned.1.call-done = bf16[128,256]{1,0:T(8,128)(2,1)} async-done(((bf16[512,256]{1,0:T(8,128)(2,1)}), bf16[128,256]{1,0:T(8,128)(2,1)}) %reduce-scatter.4.cloned.1.call-update) | async-done | bytes 65552
  247.5 66.0 %all-reduce.3.cloned.1.call-done = (f32[64,2048]{1,0:T(8,128)}, f32[64,512]{1,0:T(8,128)}) async-done(((f32[64,2048]{1,0:T(8,128)}, f32[64,512]{1,0:T(8,128)}), (f32[64,2048]{1,0:T(8,128)}, f32[64,512]{1,0:T(8,128)})) %all-reduce.3.cloned.1.call-update) | async-done | bytes 655376 | tf_op jit(solution)/shard_map/psum | solution.py:233
  313.6 1.5 divide_subtract_fusion
  315.1 1.4 divide_subtract_fusion.1
  (259 shorter events, 110.3 us)
Async XLA Ops:
  8.0 64.7 %copy-start = (bf16[256,2048]{1,0:T(8,128)(2,1)S(1)}, bf16[256,2048]{1,0:T(8,128)(2,1)}, u32[]{:S(2)}) copy-start(bf16[256,2048]{1,0:T(8,128)(2,1)} %param.22) | copy-start | bytes 3145732
  8.0 237.9 %reduce-scatter.4.cloned.1.call-start = ((), (), s32[]{:S(2)}) async-start(), calls=%async_computation.1 | async-start | bytes 327680
  8.2 33.8 %copy-start.8 = (f32[8,2048]{1,0:T(8,128)S(1)}, f32[8,2048]{1,0:T(8,128)}, u32[]{:S(2)}) copy-start(f32[8,2048]{1,0:T(8,128)} %param.23) | copy-start | bytes 196612
  8.9 32.4 %copy-start.26 = (s32[2,64]{1,0:T(2,128)S(1)}, s32[2,64]{1,0:T(2,128)}, u32[]{:S(2)}) copy-start(s32[2,64]{1,0:T(2,128)} %param.29) | copy-start | bytes 1540
  41.4 42.1 %copy-start.10 = (bf16[64,512]{1,0:T(8,128)(2,1)}, bf16[64,512]{1,0:T(8,128)(2,1)S(1)}, u32[]{:S(2)}) copy-start(bf16[64,512]{1,0:T(8,128)(2,1)S(1)} %all_gather.7) | copy-start | bytes 196612
  42.0 41.5 %copy-start.24 = (bf16[64]{0:T(256)(128)(2,1)}, bf16[64]{0:T(256)(128)(2,1)S(1)}, u32[]{:S(2)}) copy-start(bf16[64]{0:T(256)(128)(2,1)S(1)} %get-tuple-element.1761) | copy-start | bytes 388
  72.7 10.8 %copy-start.28 = (bf16[256,512]{1,0:T(8,128)(2,1)S(1)}, bf16[256,512]{1,0:T(8,128)(2,1)}, u32[]{:S(2)}) copy-start(bf16[256,512]{1,0:T(8,128)(2,1)} %param.19) | copy-start | bytes 786436
  84.0 8.8 %copy-start.4 = (bf16[256,512]{1,0:T(8,128)(2,1)}, bf16[256,512]{1,0:T(8,128)(2,1)S(1)}, u32[]{:S(2)}) copy-start(bf16[256,512]{1,0:T(8,128)(2,1)S(1)} %fusion.66) | copy-start | bytes 786436
  84.8 7.4 %copy-start.16 = (bf16[256,512]{1,0:T(8,128)(2,1)S(1)}, bf16[256,512]{1,0:T(8,128)(2,1)}, u32[]{:S(2)}) copy-start(bf16[256,512]{1,0:T(8,128)(2,1)} %param.20) | copy-start | bytes 786436
  95.2 8.3 %collective-permute-start = (bf16[256,256]{1,0:T(8,128)(2,1)S(1)}, bf16[256,256]{1,0:T(8,128)(2,1)S(1)}, u32[]{:S(2)}, u32[]{:S(2)}) collective-permute-start(bf16[256,256]{1,0:T(8,128)(2,1)S(1)} %copy.111), channel_id=1, source_target_pairs={{0,4},{4,8},{8,12},{12,16},{16,20},{20,24},{24,28},{28,0},{1,5},{5... | collective-permute-start | bytes 393224 | tf_op jit(solution)/shard_map/while/body/eval_jaxpr/ppermute | solution.py:23
  103.5 7.7 %collective-permute-start = (bf16[256,256]{1,0:T(8,128)(2,1)S(1)}, bf16[256,256]{1,0:T(8,128)(2,1)S(1)}, u32[]{:S(2)}, u32[]{:S(2)}) collective-permute-start(bf16[256,256]{1,0:T(8,128)(2,1)S(1)} %copy.111), channel_id=1, source_target_pairs={{0,4},{4,8},{8,12},{12,16},{16,20},{20,24},{24,28},{28,0},{1,5},{5... | collective-permute-start | bytes 393224 | tf_op jit(solution)/shard_map/while/body/eval_jaxpr/ppermute | solution.py:23
  111.2 7.7 %collective-permute-start = (bf16[256,256]{1,0:T(8,128)(2,1)S(1)}, bf16[256,256]{1,0:T(8,128)(2,1)S(1)}, u32[]{:S(2)}, u32[]{:S(2)}) collective-permute-start(bf16[256,256]{1,0:T(8,128)(2,1)S(1)} %copy.111), channel_id=1, source_target_pairs={{0,4},{4,8},{8,12},{12,16},{16,20},{20,24},{24,28},{28,0},{1,5},{5... | collective-permute-start | bytes 393224 | tf_op jit(solution)/shard_map/while/body/eval_jaxpr/ppermute | solution.py:23
  119.0 7.7 %collective-permute-start = (bf16[256,256]{1,0:T(8,128)(2,1)S(1)}, bf16[256,256]{1,0:T(8,128)(2,1)S(1)}, u32[]{:S(2)}, u32[]{:S(2)}) collective-permute-start(bf16[256,256]{1,0:T(8,128)(2,1)S(1)} %copy.111), channel_id=1, source_target_pairs={{0,4},{4,8},{8,12},{12,16},{16,20},{20,24},{24,28},{28,0},{1,5},{5... | collective-permute-start | bytes 393224 | tf_op jit(solution)/shard_map/while/body/eval_jaxpr/ppermute | solution.py:23
  173.7 5.2 %collective-permute-start.1 = (bf16[256,256]{0,1:T(8,128)(2,1)}, bf16[256,256]{0,1:T(8,128)(2,1)S(1)}, u32[]{:S(2)}, u32[]{:S(2)}) collective-permute-start(bf16[256,256]{0,1:T(8,128)(2,1)} %fusion.158), channel_id=1, source_target_pairs={{0,28},{4,0},{8,4},{12,8},{16,12},{20,16},{24,20},{28,24},{1,29},{... | collective-permute-start | bytes 393224 | tf_op jit(solution)/shard_map/while/body/eval_jaxpr/ppermute | solution.py:23
  185.3 7.5 %collective-permute-start.1 = (bf16[256,256]{0,1:T(8,128)(2,1)}, bf16[256,256]{0,1:T(8,128)(2,1)S(1)}, u32[]{:S(2)}, u32[]{:S(2)}) collective-permute-start(bf16[256,256]{0,1:T(8,128)(2,1)} %fusion.158), channel_id=1, source_target_pairs={{0,28},{4,0},{8,4},{12,8},{16,12},{20,16},{24,20},{28,24},{1,29},{... | collective-permute-start | bytes 393224 | tf_op jit(solution)/shard_map/while/body/eval_jaxpr/ppermute | solution.py:23
  199.2 7.9 %collective-permute-start.1 = (bf16[256,256]{0,1:T(8,128)(2,1)}, bf16[256,256]{0,1:T(8,128)(2,1)S(1)}, u32[]{:S(2)}, u32[]{:S(2)}) collective-permute-start(bf16[256,256]{0,1:T(8,128)(2,1)} %fusion.158), channel_id=1, source_target_pairs={{0,28},{4,0},{8,4},{12,8},{16,12},{20,16},{24,20},{28,24},{1,29},{... | collective-permute-start | bytes 393224 | tf_op jit(solution)/shard_map/while/body/eval_jaxpr/ppermute | solution.py:23
  213.5 7.9 %collective-permute-start.1 = (bf16[256,256]{0,1:T(8,128)(2,1)}, bf16[256,256]{0,1:T(8,128)(2,1)S(1)}, u32[]{:S(2)}, u32[]{:S(2)}) collective-permute-start(bf16[256,256]{0,1:T(8,128)(2,1)} %fusion.158), channel_id=1, source_target_pairs={{0,28},{4,0},{8,4},{12,8},{16,12},{20,16},{24,20},{28,24},{1,29},{... | collective-permute-start | bytes 393224 | tf_op jit(solution)/shard_map/while/body/eval_jaxpr/ppermute | solution.py:23
  224.4 89.2 %all-reduce.3.cloned.1.call-start = ((), (), s32[]{:S(2)}) async-start(), calls=%async_computation.2 | async-start | bytes 1310720 | tf_op jit(solution)/shard_map/psum | solution.py:233
  226.4 10.4 %copy-start.13 = (bf16[256,64]{0,1:T(8,128)(2,1)S(1)}, bf16[256,64]{0,1:T(8,128)(2,1)}, u32[]{:S(2)}) copy-start(bf16[256,64]{0,1:T(8,128)(2,1)} %copy-done.12) | copy-start | bytes 98308
  246.8 66.7 %copy-start.9 = (f32[8,2048]{1,0:T(8,128)S(1)}, f32[8,2048]{1,0:T(8,128)}, u32[]{:S(2)}) copy-start(f32[8,2048]{1,0:T(8,128)} %param.23) | copy-start | bytes 196612
  246.9 66.7 %copy-start.17 = (f32[8,2048]{1,0:T(8,128)S(1)}, f32[8,2048]{1,0:T(8,128)}, u32[]{:S(2)}) copy-start(f32[8,2048]{1,0:T(8,128)} %param.24) | copy-start | bytes 196612
  246.9 66.7 %copy-start.18 = (f32[8,2048]{1,0:T(8,128)S(1)}, f32[8,2048]{1,0:T(8,128)}, u32[]{:S(2)}) copy-start(f32[8,2048]{1,0:T(8,128)} %param.25) | copy-start | bytes 196612
  313.5 1.6 copy-start.15
  313.6 1.6 copy-start.19
  (24 other events, 20.5 us)
Sparse Core Ops, SparseCore 0:
  224.5 21.3 reduce-scatter.3
Sparse Core Ops, SparseCore 1:
  238.9 74.6 all-reduce.2
where the time goes:
time: 326 us; the launch traced here: 324 us
  waiting for transfers between devices  91 us (28%)
  blocking collectives  83.8 us (26%)
  other arithmetic  50.3 us (15%)
  local copies, waits for them, and re-layouts  33.2 us (10%)
  matrix products  29.5 us (9%)
  starting transfers between devices  18.6 us (6%)
  between operations  16.6 us (5%)
    psum x1, waiting for transfers between devices, on_device(): sum_down, sum_up = lax.psum((part_down, partial_up), 'ctx')  66 us
    all_gather x1, blocking collectives, on_device(): lax.all_gather(adapter_up.astype(jnp.bfloat16), 'ctx', axis=0, tiled=True)  32.4 us
    all_gather x1, blocking collectives, on_device(): lax.all_gather(adapter_down.astype(jnp.bfloat16), 'ctx', axis=0, tiled=True)  30.7 us
    ppermute x8, waiting for transfers between devices, shifted(): return lax.ppermute(value, axis, pairs)  20.4 us
    select_n x15, other arithmetic, tile_scores(): key_rolled // group_here  19.5 us
    ppermute x8, starting transfers between devices, shifted(): return lax.ppermute(value, axis, pairs)  18.5 us
    select_n x14, other arithmetic, on_device(): query_group = query_rolled // group_here  18.2 us
    dot_general x15, matrix products, tile_scores(): jnp.einsum('qhd,kd->hqk', query_heads, pair_rows[:, :HEAD_SIZE], preferre...  15.2 us
  transfers between devices with their start and end apart: 10, of which 10 were waited for; matrix products, arithmetic and copies ran while one was open for 8% of the time, Pallas kernels for 0%

commit v1 on v0

--- a/solution.py
+++ b/solution.py
@@ -1,8 +1,11 @@
+import functools
 import math
 
 import jax
 import jax.numpy as jnp
 from jax import lax
+from jax.experimental import pallas as pl
+from jax.experimental.pallas import tpu as pltpu
 from jax.sharding import PartitionSpec as P
 
 LOCAL_HEADS = 16
@@ -256,6 +259,486 @@
     )
 
 
+CONTRACT_LAST = (((1,), (1,)), ((), ()))
+CONTRACT_FIRST = (((0,), (0,)), ((), ()))
+
+
+def matmul(left, right, dims=(((1,), (0,)), ((), ()))):
+    return lax.dot_general(left, right, dims, preferred_element_type=jnp.float32)
+
+
+def remote(source, target, send_sem, recv_sem, device):
+    return pltpu.make_async_remote_copy(
+        src_ref=source,
+        dst_ref=target,
+        send_sem=send_sem,
+        recv_sem=recv_sem,
+        device_id=device,
+        device_id_type=pl.DeviceIdType.MESH,
+    )
+
+
+def fused_kernel(
+    ctx_count,
+    frozen_ref,
+    rows_ref,
+    cotangent_ref,
+    inputs_ref,
+    down_ref,
+    down_one_ref,
+    down_two_ref,
+    up_ref,
+    up_one_ref,
+    up_two_ref,
+    mask_ref,
+    length_ref,
+    shift_ref,
+    out_ref,
+    query_grad_ref,
+    kv_grad_ref,
+    new_down_ref,
+    new_down_one_ref,
+    new_down_two_ref,
+    new_up_ref,
+    new_up_one_ref,
+    new_up_two_ref,
+    factors,
+    down_full,
+    up_full,
+    pairs,
+    proj_parts,
+    rank_parts,
+    weight_rows,
+    score_rows,
+    query_columns,
+    grad_columns,
+    own_part,
+    core_send,
+    core_parts,
+    owner_send,
+    owner_parts,
+    sum_send,
+    sum_parts,
+    send_sems,
+    factor_sems,
+    pair_sems,
+    proj_sems,
+    rank_sems,
+    core_sems,
+    owner_sems,
+    sum_sems,
+):
+    tokens = frozen_ref.shape[0]
+    half = tokens // 2
+    heads = frozen_ref.shape[1] // HEAD_SIZE
+    reach = pairs.shape[0] - 1
+    head_count = proj_parts.shape[0]
+    local_rows = down_ref.shape[0]
+    down_half = down_ref.shape[1] // 2
+    up_half = up_ref.shape[1] // 2
+    seq_total = tokens * ctx_count
+    key_width = KVH * HEAD_SIZE
+    score_scale = 1.0 / math.sqrt(HEAD_SIZE)
+    place = lax.axis_index("ctx")
+    lane = lax.axis_index("head")
+    chip = lane // 2
+    core = lane % 2
+    odd = place % 2
+    beside = place + 1 - 2 * odd
+    other_core = lane + 1 - 2 * core
+    final_lane = core * 2 + chip
+    crossing = chip != core
+    used = [0]
+    sent = []
+
+    def next_sem():
+        used[0] += 1
+        return send_sems.at[used[0] - 1]
+
+    def away(steps):
+        return lax.rem(place + steps + ctx_count, ctx_count)
+
+    def send(source, target, recv_sem, device, when=None):
+        copy = remote(source, target, next_sem(), recv_sem, device)
+        if when is None:
+            copy.start()
+        else:
+            pl.when(when)(copy.start)
+        sent.append((copy, when))
+
+    def arrived(target, recv_sem):
+        remote(target, target, send_sems.at[0], recv_sem, (place, lane)).wait_recv()
+
+    barrier = pltpu.get_barrier_semaphore()
+
+    def greet(device):
+        pl.semaphore_signal(
+            barrier, inc=1, device_id=device, device_id_type=pl.DeviceIdType.MESH
+        )
+
+    for steps in range(1, ctx_count):
+        greet((away(steps), lane))
+    for steps in range(1, head_count):
+        greet((place, lax.rem(lane + steps, head_count)))
+
+    @pl.when(crossing)
+    def _():
+        for steps in range(1, ctx_count):
+            greet((away(steps), final_lane))
+
+    own_down = down_ref[...]
+    own_up = up_ref[...]
+    factors[place] = jnp.concatenate(
+        [
+            jnp.concatenate([own_down[:, :down_half], own_down[:, down_half:]], 0),
+            jnp.concatenate([own_up[:, :up_half], own_up[:, up_half:]], 0),
+        ],
+        1,
+    ).astype(jnp.bfloat16)
+    key_start = pl.multiple_of(chip * HEAD_SIZE, HEAD_SIZE)
+    pairs[0, :, :HEAD_SIZE] = rows_ref[:, pl.ds(key_start, HEAD_SIZE)]
+    pairs[0, :, HEAD_SIZE:] = rows_ref[:, pl.ds(key_width + key_start, HEAD_SIZE)]
+
+    straight_peers = ctx_count + head_count - 2
+
+    @pl.when(crossing)
+    def _():
+        pl.semaphore_wait(barrier, straight_peers + ctx_count - 1)
+
+    @pl.when(jnp.logical_not(crossing))
+    def _():
+        pl.semaphore_wait(barrier, straight_peers)
+
+    def send_factors(owner, device_place):
+        send(
+            factors.at[owner], factors.at[owner], factor_sems.at[owner], (device_place, lane)
+        )
+
+    half_start = pl.multiple_of(core * half, half)
+
+    def pair_half(slot, start):
+        return pairs.at[slot, pl.ds(start, half)]
+
+    def send_pair(slot, new_slot, device, when=None):
+        send(
+            pair_half(slot, half_start),
+            pair_half(new_slot, half_start),
+            pair_sems.at[new_slot, core],
+            device,
+            when,
+        )
+
+    for steps in range(2, ctx_count, 2):
+        send_factors(place, away(steps))
+    send_factors(place, beside)
+    send_pair(0, 2, (away(2), lane))
+    send_pair(0, 4, (away(4), lane))
+    send_pair(0, 1, (beside, lane), odd == 0)
+    for steps in range(2, ctx_count, 2):
+        owner = away(steps)
+        arrived(factors.at[owner], factor_sems.at[owner])
+        send_factors(owner, beside)
+
+    core_device = (place, other_core)
+    arrived(pair_half(2, half_start), pair_sems.at[2, core])
+    send_pair(2, 3, (beside, lane), odd == 0)
+    send_pair(2, 1, (beside, lane), odd == 1)
+    send_pair(2, 2, core_device)
+    arrived(pair_half(4, half_start), pair_sems.at[4, core])
+    send_pair(4, 3, (beside, lane), odd == 1)
+    send_pair(4, 4, core_device)
+
+    for steps in range(0, ctx_count, 2):
+        owner = lax.rem(beside + steps, ctx_count)
+        arrived(factors.at[owner], factor_sems.at[owner])
+
+    mask_rows = mask_ref[...].astype(jnp.float32)
+    rank_all = mask_rows.shape[1]
+    diagonal = lax.broadcasted_iota(jnp.int32, (rank_all, rank_all), 0) == (
+        lax.broadcasted_iota(jnp.int32, (rank_all, rank_all), 1)
+    )
+
+    def column(row):
+        return jnp.sum(jnp.where(diagonal, row, 0.0), 1, keepdims=True)
+
+    down_keep = column(mask_rows[0:1])
+    up_keep = column(mask_rows[1:2])
+    for owner in range(ctx_count):
+        block = factors[owner].astype(jnp.float32)
+        rows = slice(owner * local_rows, (owner + 1) * local_rows)
+        down_full[rows, :down_half] = block[:local_rows, :down_half]
+        down_full[rows, down_half:] = block[local_rows:, :down_half]
+        up_full[rows, :up_half] = block[:local_rows, down_half:]
+        up_full[rows, up_half:] = block[local_rows:, down_half:]
+    masked_up = (up_full[...] * up_keep).astype(jnp.bfloat16)
+    proj_parts[lane] = matmul(
+        down_full[...].astype(jnp.bfloat16), inputs_ref[...], CONTRACT_LAST
+    ).astype(jnp.bfloat16)
+
+    def send_to_heads(parts, sems):
+        for steps in range(1, head_count):
+            send(
+                parts.at[lane],
+                parts.at[lane],
+                sems.at[lane],
+                (place, lax.rem(lane + steps, head_count)),
+            )
+
+    def sum_of_heads(parts, sems):
+        for steps in range(1, head_count):
+            source = lax.rem(lane + steps, head_count)
+            arrived(parts.at[source], sems.at[source])
+        total = parts[0].astype(jnp.float32)
+        for source in range(1, head_count):
+            total = total + parts[source].astype(jnp.float32)
+        return total
+
+    send_to_heads(proj_parts, proj_sems)
+    for slot in (1, 3):
+        arrived(pair_half(slot, half_start), pair_sems.at[slot, core])
+        send_pair(slot, slot, core_device)
+    other_start = pl.multiple_of((1 - core) * half, half)
+    for slot in range(1, reach + 1):
+        arrived(pair_half(slot, other_start), pair_sems.at[slot, 1 - core])
+    for head in range(heads):
+        grad_columns[:, head * tokens : (head + 1) * tokens] = (
+            cotangent_ref[:, head * HEAD_SIZE : (head + 1) * HEAD_SIZE].astype(jnp.float32).T
+        ).astype(jnp.bfloat16)
+
+    length = length_ref[chip]
+    first_rolled = lax.rem(place * tokens - shift_ref[chip] + seq_total, seq_total)
+    first_inside = lax.rem(first_rolled, length)
+    query_index = lax.broadcasted_iota(jnp.int32, (tokens, 1), 0)
+    inside = first_inside + query_index
+    inside = jnp.where(inside >= length, inside - length, inside)
+    rolled = first_rolled + query_index
+    inside = jnp.where(rolled >= seq_total, rolled - seq_total, inside)
+    gap = lax.broadcasted_iota(jnp.int32, (tokens, tokens), 0) - lax.broadcasted_iota(
+        jnp.int32, (tokens, tokens), 1
+    )
+    lower = gap >= 0
+    allowed = [jnp.where(lower, gap, gap + reach * tokens) <= inside]
+    for slot in range(1, reach):
+        allowed.append(gap + slot * tokens <= inside)
+
+    masked_proj = (sum_of_heads(proj_parts, proj_sems) * (down_keep * up_keep)).astype(
+        jnp.bfloat16
+    )
+    span = (reach + 1) * tokens
+    all_keys = pairs[:, :, :HEAD_SIZE].reshape(span, HEAD_SIZE)
+    all_values = pairs[:, :, HEAD_SIZE:].reshape(span, HEAD_SIZE)
+
+    def tiles_of(product):
+        first = jnp.where(lower, product[:, :tokens], product[:, reach * tokens :])
+        return [first] + [
+            product[:, slot * tokens : (slot + 1) * tokens] for slot in range(1, reach)
+        ]
+
+    def spread(tiles):
+        nothing = jnp.zeros_like(tiles[0])
+        return jnp.concatenate(
+            [jnp.where(lower, tiles[0], nothing)]
+            + tiles[1:]
+            + [jnp.where(lower, nothing, tiles[0])],
+            1,
+        ).astype(jnp.bfloat16)
+
+    for head in range(heads):
+        columns = slice(head * HEAD_SIZE, (head + 1) * HEAD_SIZE)
+        rows = slice(head * tokens, (head + 1) * tokens)
+        query = (
+            frozen_ref[:, columns].astype(jnp.float32)
+            + adapter_scale * matmul(masked_proj, masked_up[:, columns], CONTRACT_FIRST)
+        )
+        query_columns[:, rows] = query.astype(jnp.bfloat16).astype(jnp.float32).T.astype(
+            jnp.bfloat16
+        )
+        query = query.astype(jnp.bfloat16)
+        scores = [
+            jnp.where(keep, tile * score_scale, -1e30)
+            for keep, tile in zip(allowed, tiles_of(matmul(query, all_keys, CONTRACT_LAST)))
+        ]
+        row_max = jnp.max(
+            jnp.maximum(jnp.maximum(scores[0], scores[1]), jnp.maximum(scores[2], scores[3])),
+            1,
+            keepdims=True,
+        )
+        powers = [jnp.exp(tile - row_max) for tile in scores]
+        total = jnp.sum(powers[0] + powers[1] + powers[2] + powers[3], 1, keepdims=True)
+        inverse = 1.0 / total
+        weights = [tile * inverse for tile in powers]
+        grad_weights = tiles_of(matmul(cotangent_ref[:, columns], all_values, CONTRACT_LAST))
+        products = [tile * grad for tile, grad in zip(weights, grad_weights)]
+        row_dots = jnp.sum(
+            products[0] + products[1] + products[2] + products[3], 1, keepdims=True
+        )
+        grad_scores = spread(
+            [tile * (grad - row_dots) for tile, grad in zip(weights, grad_weights)]
+        )
+        weights_half = spread(weights)
+        weight_rows[rows, :] = weights_half
+        score_rows[rows, :] = grad_scores
+        out_ref[:, columns] = matmul(weights_half, all_values).astype(jnp.bfloat16)
+        query_grad_ref[:, columns] = (score_scale * matmul(grad_scores, all_keys)).astype(
+            jnp.bfloat16
+        )
+
+    query_grad = query_grad_ref[...]
+    rank_parts[lane] = matmul(masked_up, query_grad, CONTRACT_LAST).astype(jnp.bfloat16)
+    send_to_heads(rank_parts, rank_sems)
+
+    for slot in range(reach, -1, -1):
+        keys = slice(slot * tokens, (slot + 1) * tokens)
+        key_part = score_scale * matmul(query_columns[...], score_rows[:, keys])
+        value_part = matmul(grad_columns[...], weight_rows[:, keys])
+        core_send[slot] = jnp.where(core == 0, value_part, key_part).astype(jnp.bfloat16)
+        own_part[slot] = jnp.where(core == 0, key_part, value_part)
+        send(core_send.at[slot], core_parts.at[slot], core_sems.at[slot], core_device)
+
+    up_sum = adapter_scale * matmul(masked_proj, query_grad)
+
+    for slot in range(reach, -1, -1):
+        arrived(core_parts.at[slot], core_sems.at[slot])
+        owner_send[slot] = (own_part[slot] + core_parts[slot].astype(jnp.float32)).astype(
+            jnp.bfloat16
+        )
+        send(
+            owner_send.at[slot],
+            owner_parts.at[slot],
+            owner_sems.at[slot],
+            (away(-slot), final_lane),
+            crossing if slot == 0 else None,
+        )
+
+    rank_product = (
+        sum_of_heads(rank_parts, rank_sems) * (down_keep * adapter_scale)
+    ).astype(jnp.bfloat16)
+    down_sum = matmul(rank_product, inputs_ref[...])
+    for owner in range(ctx_count):
+        rows = slice(owner * local_rows, (owner + 1) * local_rows)
+        sum_send[owner] = jnp.concatenate(
+            [
+                jnp.concatenate([down_sum[rows, :down_half], down_sum[rows, down_half:]], 0),
+                jnp.concatenate([up_sum[rows, :up_half], up_sum[rows, up_half:]], 0),
+            ],
+            1,
+        ).astype(jnp.bfloat16)
+    for steps in range(1, ctx_count):
+        owner = away(steps)
+        send(
+            sum_send.at[owner], sum_parts.at[place], sum_sems.at[place], (owner, lane)
+        )
+    gradient = sum_send[place].astype(jnp.float32)
+    for steps in range(1, ctx_count):
+        source = away(-steps)
+        arrived(sum_parts.at[source], sum_sems.at[source])
+        gradient = gradient + sum_parts[source].astype(jnp.float32)
+    down_gradient = jnp.concatenate(
+        [gradient[:local_rows, :down_half], gradient[local_rows:, :down_half]], 1
+    )
+    up_gradient = jnp.concatenate(
+        [gradient[:local_rows, down_half:], gradient[local_rows:, down_half:]], 1
+    )
+    new_down_ref[...], new_down_one_ref[...], new_down_two_ref[...] = adam_update(
+        own_down, down_one_ref[...], down_two_ref[...], down_gradient
+    )
+    new_up_ref[...], new_up_one_ref[...], new_up_two_ref[...] = adam_update(
+        own_up, up_one_ref[...], up_two_ref[...], up_gradient
+    )
+
+    @pl.when(crossing)
+    def _():
+        arrived(owner_parts.at[0], owner_sems.at[0])
+
+    @pl.when(jnp.logical_not(crossing))
+    def _():
+        owner_parts[0] = owner_send[0]
+
+    part_sum = owner_parts[0].astype(jnp.float32)
+    for slot in range(1, reach + 1):
+        arrived(owner_parts.at[slot], owner_sems.at[slot])
+        part_sum = part_sum + owner_parts[slot].astype(jnp.float32)
+    kv_grad_ref[...] = part_sum.T
+
+    for copy, when in sent:
+        if when is None:
+            copy.wait_send()
+        else:
+            pl.when(when)(copy.wait_send)
+
+
+def fused(*args):
+    frozen, rows, _, inputs, down, _, _, up = args[:8]
+    ctx_count = lax.axis_size("ctx")
+    head_count = lax.axis_size("head")
+    reach = min(8, ctx_count // 2)
+    tokens = frozen.shape[0]
+    heads = frozen.shape[1] // HEAD_SIZE
+    local_rows = down.shape[0]
+    rank_all = local_rows * ctx_count
+    block = (2 * local_rows, (down.shape[1] + up.shape[1]) // 2)
+    half_type, full_type = jnp.bfloat16, jnp.float32
+    in_vmem = pl.BlockSpec(memory_space=pltpu.VMEM)
+    in_smem = pl.BlockSpec(memory_space=pltpu.SMEM)
+    shapes = [
+        (frozen.shape, half_type),
+        (frozen.shape, half_type),
+        ((tokens, HEAD_SIZE), full_type),
+        (down.shape, full_type),
+        (down.shape, full_type),
+        (down.shape, full_type),
+        (up.shape, full_type),
+        (up.shape, full_type),
+        (up.shape, full_type),
+    ]
+    return pl.pallas_call(
+        functools.partial(fused_kernel, ctx_count),
+        out_shape=[jax.ShapeDtypeStruct(shape, kind) for shape, kind in shapes],
+        in_specs=[in_vmem] * 11 + [in_smem] * 2,
+        out_specs=[in_vmem] * 9,
+        scratch_shapes=[
+            pltpu.VMEM((ctx_count,) + block, half_type),
+            pltpu.VMEM((rank_all, down.shape[1]), full_type),
+            pltpu.VMEM((rank_all, up.shape[1]), full_type),
+            pltpu.VMEM((reach + 1, tokens, 2 * HEAD_SIZE), half_type),
+            pltpu.VMEM((head_count, rank_all, tokens), half_type),
+            pltpu.VMEM((head_count, rank_all, tokens), half_type),
+            pltpu.VMEM((heads * tokens, (reach + 1) * tokens), half_type),
+            pltpu.VMEM((heads * tokens, (reach + 1) * tokens), half_type),
+            pltpu.VMEM((HEAD_SIZE, heads * tokens), half_type),
+            pltpu.VMEM((HEAD_SIZE, heads * tokens), half_type),
+            pltpu.VMEM((reach + 1, HEAD_SIZE, tokens), full_type),
+            pltpu.VMEM((reach + 1, HEAD_SIZE, tokens), half_type),
+            pltpu.VMEM((reach + 1, HEAD_SIZE, tokens), half_type),
+            pltpu.VMEM((reach + 1, HEAD_SIZE, tokens), half_type),
+            pltpu.VMEM((reach + 1, HEAD_SIZE, tokens), half_type),
+            pltpu.VMEM((ctx_count,) + block, half_type),
+            pltpu.VMEM((ctx_count,) + block, half_type),
+            pltpu.SemaphoreType.DMA((64,)),
+            pltpu.SemaphoreType.DMA((ctx_count,)),
+            pltpu.SemaphoreType.DMA((reach + 1, 2)),
+            pltpu.SemaphoreType.DMA((head_count,)),
+            pltpu.SemaphoreType.DMA((head_count,)),
+            pltpu.SemaphoreType.DMA((reach + 1,)),
+            pltpu.SemaphoreType.DMA((reach + 1,)),
+            pltpu.SemaphoreType.DMA((ctx_count,)),
+        ],
+        compiler_params=pltpu.CompilerParams(
+            collective_id=0, has_side_effects=True, vmem_limit_bytes=40 * 1024 * 1024
+        ),
+    )(*args)
+
+
+def on_any_mesh(*args):
+    fits = (
+        min(8, lax.axis_size("ctx") // 2) == 4
+        and lax.axis_size("ctx") % 2 == 0
+        and args[4].shape[0] % 8 == 0
+        and lax.axis_size("head") == 2 * KVH
+    )
+    return tuple(fused(*args)) if fits else on_device(*args)
+
+
 def solution(mesh):
     placed = (
         P("ctx", "head"),
@@ -273,7 +756,7 @@
         P(),
     )
     return jax.shard_map(
-        on_device,
+        on_any_mesh,
         mesh=mesh,
         in_specs=placed,
         out_specs=(

time: 326 us -> 62.4 us (0.19)
  the two profiles are of different devices: /device:TPU:0 before, /device:TPU:29 now
where the time goes in v1:
time: 62.4 us; the launch traced here: 61.8 us
  Pallas kernels  44.6 us (71%)
  local copies, waits for them, and re-layouts  16.5 us (26%)
  between operations  0.68 us (1%)
    pallas_call x1, Pallas kernels, fused(): pl.pallas_call(functools.partial(fused_kernel, ctx_count), out_shape=[jax...  44.6 us
    unnamed x35, local copies, waits for them, and re-layouts  16.5 us

profile of v1, /device:TPU:29, one launch (start us, length us, event | category | flops | bytes accessed | tf_op | source)
XLA Modules:
  0.0 61.8 jit_solution(9616656595633180716)
XLA Ops:
  0.6 0.0 copy-start
  0.7 1.2 %copy-done = bf16[256,2048]{1,0:T(8,128)(2,1)S(1)} copy-done((bf16[256,2048]{1,0:T(8,128)(2,1)S(1)}, bf16[256,2048]{1,0:T(8,128)(2,1)}, u32[]{:S(2)}) %copy-start) | copy-done | bytes 1048600
  1.9 0.9 %copy-done.1 = bf16[256,512]{1,0:T(8,128)(2,1)S(1)} copy-done((bf16[256,512]{1,0:T(8,128)(2,1)S(1)}, bf16[256,512]{1,0:T(8,128)(2,1)}, u32[]{:S(2)}) %copy-start.1) | copy-done | bytes 262168
  2.8 0.9 %copy-done.2 = bf16[256,512]{1,0:T(8,128)(2,1)S(1)} copy-done((bf16[256,512]{1,0:T(8,128)(2,1)S(1)}, bf16[256,512]{1,0:T(8,128)(2,1)}, u32[]{:S(2)}) %copy-start.2) | copy-done | bytes 262168
  3.8 0.9 %copy-done.3 = bf16[256,512]{1,0:T(8,128)(2,1)S(1)} copy-done((bf16[256,512]{1,0:T(8,128)(2,1)S(1)}, bf16[256,512]{1,0:T(8,128)(2,1)}, u32[]{:S(2)}) %copy-start.3) | copy-done | bytes 262168
  4.7 0.8 %copy-done.4 = f32[8,2048]{1,0:T(8,128)S(1)} copy-done((f32[8,2048]{1,0:T(8,128)S(1)}, f32[8,2048]{1,0:T(8,128)}, u32[]{:S(2)}) %copy-start.4) | copy-done | bytes 65560
  5.6 0.8 %copy-done.5 = f32[8,2048]{1,0:T(8,128)S(1)} copy-done((f32[8,2048]{1,0:T(8,128)S(1)}, f32[8,2048]{1,0:T(8,128)}, u32[]{:S(2)}) %copy-start.5) | copy-done | bytes 65560
  6.4 0.8 %copy-done.6 = f32[8,2048]{1,0:T(8,128)S(1)} copy-done((f32[8,2048]{1,0:T(8,128)S(1)}, f32[8,2048]{1,0:T(8,128)}, u32[]{:S(2)}) %copy-start.6) | copy-done | bytes 65560
  7.2 0.7 %copy-done.7 = f32[8,512]{1,0:T(8,128)S(1)} copy-done((f32[8,512]{1,0:T(8,128)S(1)}, f32[8,512]{1,0:T(8,128)}, u32[]{:S(2)}) %copy-start.7) | copy-done | bytes 16408
  8.0 0.7 %copy-done.8 = f32[8,512]{1,0:T(8,128)S(1)} copy-done((f32[8,512]{1,0:T(8,128)S(1)}, f32[8,512]{1,0:T(8,128)}, u32[]{:S(2)}) %copy-start.8) | copy-done | bytes 16408
  8.7 0.7 %copy-done.9 = f32[8,512]{1,0:T(8,128)S(1)} copy-done((f32[8,512]{1,0:T(8,128)S(1)}, f32[8,512]{1,0:T(8,128)}, u32[]{:S(2)}) %copy-start.9) | copy-done | bytes 16408
  9.4 0.7 %copy-done.10 = s32[2,64]{1,0:T(2,128)S(1)} copy-done((s32[2,64]{1,0:T(2,128)S(1)}, s32[2,64]{1,0:T(2,128)}, u32[]{:S(2)}) %copy-start.10) | copy-done | bytes 536
  10.1 0.7 %copy-done.11 = s32[2]{0:T(128)S(1)} copy-done((s32[2]{0:T(128)S(1)}, s32[2]{0:T(128)}, u32[]{:S(2)}) %copy-start.11) | copy-done | bytes 32
  10.7 0.7 %copy-done.12 = s32[2]{0:T(128)S(1)} copy-done((s32[2]{0:T(128)S(1)}, s32[2]{0:T(128)}, u32[]{:S(2)}) %copy-start.12) | copy-done | bytes 32
  11.4 44.6 %shard_map.196 = (bf16[256,512]{1,0:T(8,128)(2,1)S(1)}, bf16[256,512]{1,0:T(8,128)(2,1)S(1)}, f32[256,128]{1,0:T(8,128)S(1)}, f32[8,2048]{1,0:T(8,128)S(1)}, f32...) custom-call(bf16[256,512]{1,0:T(8,128)(2,1)S(1)} %copy-done.1, ...), custom_call_target="tpu_custom_call" | custom-call | tf_op jit(solution)/shard_map/pallas_call | solution.py:694
  56.0 0.7 %copy.31 = bf16[256,512]{1,0:T(8,128)(2,1)} copy(bf16[256,512]{1,0:T(8,128)(2,1)S(1)} %get-tuple-element.18) | data formatting | bytes 524288
  56.7 0.7 %copy.32 = bf16[256,512]{1,0:T(8,128)(2,1)} copy(bf16[256,512]{1,0:T(8,128)(2,1)S(1)} %get-tuple-element.19) | data formatting | bytes 524288
  57.4 0.7 %copy.33 = f32[256,128]{1,0:T(8,128)} copy(f32[256,128]{1,0:T(8,128)S(1)} %get-tuple-element.20) | data formatting | bytes 262144
  58.1 0.6 %copy.34 = f32[8,2048]{1,0:T(8,128)} copy(f32[8,2048]{1,0:T(8,128)S(1)} %get-tuple-element.21) | data formatting | bytes 131072
  58.7 0.6 %copy.35 = f32[8,2048]{1,0:T(8,128)} copy(f32[8,2048]{1,0:T(8,128)S(1)} %get-tuple-element.22) | data formatting | bytes 131072
  59.3 0.6 %copy.36 = f32[8,2048]{1,0:T(8,128)} copy(f32[8,2048]{1,0:T(8,128)S(1)} %get-tuple-element.23) | data formatting | bytes 131072
  60.0 0.6 copy.37
  60.6 0.6 copy.38
  61.2 0.6 copy.39
  (12 shorter events, 0.0 us)
Async XLA Ops:
  0.6 1.2 %copy-start = (bf16[256,2048]{1,0:T(8,128)(2,1)S(1)}, bf16[256,2048]{1,0:T(8,128)(2,1)}, u32[]{:S(2)}) copy-start(bf16[256,2048]{1,0:T(8,128)(2,1)} %inputs_ref.1) | copy-start | bytes 3145732
  1.9 0.9 %copy-start.1 = (bf16[256,512]{1,0:T(8,128)(2,1)S(1)}, bf16[256,512]{1,0:T(8,128)(2,1)}, u32[]{:S(2)}) copy-start(bf16[256,512]{1,0:T(8,128)(2,1)} %frozen_ref.1) | copy-start | bytes 786436
  2.8 0.9 %copy-start.2 = (bf16[256,512]{1,0:T(8,128)(2,1)S(1)}, bf16[256,512]{1,0:T(8,128)(2,1)}, u32[]{:S(2)}) copy-start(bf16[256,512]{1,0:T(8,128)(2,1)} %rows_ref.1) | copy-start | bytes 786436
  3.8 0.9 %copy-start.3 = (bf16[256,512]{1,0:T(8,128)(2,1)S(1)}, bf16[256,512]{1,0:T(8,128)(2,1)}, u32[]{:S(2)}) copy-start(bf16[256,512]{1,0:T(8,128)(2,1)} %cotangent_ref.1) | copy-start | bytes 786436
  4.7 0.8 %copy-start.4 = (f32[8,2048]{1,0:T(8,128)S(1)}, f32[8,2048]{1,0:T(8,128)}, u32[]{:S(2)}) copy-start(f32[8,2048]{1,0:T(8,128)} %down_ref.1) | copy-start | bytes 196612
  5.6 0.8 %copy-start.5 = (f32[8,2048]{1,0:T(8,128)S(1)}, f32[8,2048]{1,0:T(8,128)}, u32[]{:S(2)}) copy-start(f32[8,2048]{1,0:T(8,128)} %down_one_ref.1) | copy-start | bytes 196612
  6.4 0.8 %copy-start.6 = (f32[8,2048]{1,0:T(8,128)S(1)}, f32[8,2048]{1,0:T(8,128)}, u32[]{:S(2)}) copy-start(f32[8,2048]{1,0:T(8,128)} %down_two_ref.1) | copy-start | bytes 196612
  7.2 0.7 %copy-start.7 = (f32[8,512]{1,0:T(8,128)S(1)}, f32[8,512]{1,0:T(8,128)}, u32[]{:S(2)}) copy-start(f32[8,512]{1,0:T(8,128)} %up_ref.1) | copy-start | bytes 49156
  8.0 0.7 %copy-start.8 = (f32[8,512]{1,0:T(8,128)S(1)}, f32[8,512]{1,0:T(8,128)}, u32[]{:S(2)}) copy-start(f32[8,512]{1,0:T(8,128)} %up_one_ref.1) | copy-start | bytes 49156
  8.7 0.7 %copy-start.9 = (f32[8,512]{1,0:T(8,128)S(1)}, f32[8,512]{1,0:T(8,128)}, u32[]{:S(2)}) copy-start(f32[8,512]{1,0:T(8,128)} %up_two_ref.1) | copy-start | bytes 49156
  9.4 0.7 %copy-start.10 = (s32[2,64]{1,0:T(2,128)S(1)}, s32[2,64]{1,0:T(2,128)}, u32[]{:S(2)}) copy-start(s32[2,64]{1,0:T(2,128)} %mask_ref.1) | copy-start | bytes 1540
  10.1 0.7 %copy-start.11 = (s32[2]{0:T(128)S(1)}, s32[2]{0:T(128)}, u32[]{:S(2)}) copy-start(s32[2]{0:T(128)} %length_ref.1) | copy-start | bytes 28
  10.7 0.7 %copy-start.12 = (s32[2]{0:T(128)S(1)}, s32[2]{0:T(128)}, u32[]{:S(2)}) copy-start(s32[2]{0:T(128)} %shift_ref.1) | copy-start | bytes 28

commit v2 on v1

--- a/solution.py
+++ b/solution.py
@@ -259,6 +259,7 @@
     )
 
 
+VMEM_GRANT = 62 * 1024 * 1024
 CONTRACT_LAST = (((1,), (1,)), ((), ()))
 CONTRACT_FIRST = (((0,), (0,)), ((), ()))
 
@@ -278,8 +279,9 @@
     )
 
 
-def fused_kernel(
+def layer_body(
     ctx_count,
+    ready,
     frozen_ref,
     rows_ref,
     cotangent_ref,
@@ -317,8 +319,10 @@
     core_parts,
     owner_send,
     owner_parts,
+    beside_parts,
     sum_send,
     sum_parts,
+    sum_beside,
     send_sems,
     factor_sems,
     pair_sems,
@@ -326,7 +330,9 @@
     rank_sems,
     core_sems,
     owner_sems,
+    beside_sems,
     sum_sems,
+    sum_beside_sems,
 ):
     tokens = frozen_ref.shape[0]
     half = tokens // 2
@@ -386,6 +392,7 @@
         for steps in range(1, ctx_count):
             greet((away(steps), final_lane))
 
+    ready(4, 7, 1)
     own_down = down_ref[...]
     own_up = up_ref[...]
     factors[place] = jnp.concatenate(
@@ -452,6 +459,7 @@
         owner = lax.rem(beside + steps, ctx_count)
         arrived(factors.at[owner], factor_sems.at[owner])
 
+    ready(10, 3, 2)
     mask_rows = mask_ref[...].astype(jnp.float32)
     rank_all = mask_rows.shape[1]
     diagonal = lax.broadcasted_iota(jnp.int32, (rank_all, rank_all), 0) == (
@@ -505,6 +513,7 @@
             cotangent_ref[:, head * HEAD_SIZE : (head + 1) * HEAD_SIZE].astype(jnp.float32).T
         ).astype(jnp.bfloat16)
 
+    ready(11, 12, 0)
     length = length_ref[chip]
     first_rolled = lax.rem(place * tokens - shift_ref[chip] + seq_total, seq_total)
     first_inside = lax.rem(first_rolled, length)
@@ -587,7 +596,8 @@
     rank_parts[lane] = matmul(masked_up, query_grad, CONTRACT_LAST).astype(jnp.bfloat16)
     send_to_heads(rank_parts, rank_sems)
 
-    for slot in range(reach, -1, -1):
+    slots = (3, 1, 4, 2, 0)
+    for slot in slots:
         keys = slice(slot * tokens, (slot + 1) * tokens)
         key_part = score_scale * matmul(query_columns[...], score_rows[:, keys])
         value_part = matmul(grad_columns[...], weight_rows[:, keys])
@@ -597,17 +607,17 @@
 
     up_sum = adapter_scale * matmul(masked_proj, query_grad)
 
-    for slot in range(reach, -1, -1):
+    def chip_sum(slot):
         arrived(core_parts.at[slot], core_sems.at[slot])
-        owner_send[slot] = (own_part[slot] + core_parts[slot].astype(jnp.float32)).astype(
-            jnp.bfloat16
-        )
+        return own_part[slot] + core_parts[slot].astype(jnp.float32)
+
+    for index, slot in ((1, 3), (0, 1)):
+        owner_send[slot] = chip_sum(slot).astype(jnp.bfloat16)
         send(
             owner_send.at[slot],
-            owner_parts.at[slot],
-            owner_sems.at[slot],
-            (away(-slot), final_lane),
-            crossing if slot == 0 else None,
+            beside_parts.at[index],
+            beside_sems.at[index],
+            (beside, lane),
         )
 
     rank_product = (
@@ -623,14 +633,57 @@
             ],
             1,
         ).astype(jnp.bfloat16)
-    for steps in range(1, ctx_count):
-        owner = away(steps)
+    pair_count = ctx_count // 2
+    pair_place = place // 2
+
+    def pair_away(steps):
+        return lax.rem(pair_place + steps + pair_count, pair_count)
+
+    for steps in range(1, pair_count + 1):
+        owner_pair = pair_away(steps)
         send(
-            sum_send.at[owner], sum_parts.at[place], sum_sems.at[place], (owner, lane)
-        )
-    gradient = sum_send[place].astype(jnp.float32)
-    for steps in range(1, ctx_count):
-        source = away(-steps)
+            sum_send.at[2 * owner_pair + 1 - odd],
+            sum_beside.at[owner_pair],
+            sum_beside_sems.at[owner_pair],
+            (beside, lane),
+        )
+
+    arrived(beside_parts.at[1], beside_sems.at[1])
+    far_extra = beside_parts[1].astype(jnp.float32)
+    owner_send[4] = (chip_sum(4) + jnp.where(odd == 1, far_extra, 0.0)).astype(jnp.bfloat16)
+    send(
+        owner_send.at[4], owner_parts.at[2], owner_sems.at[2], (away(-4), final_lane)
+    )
+    arrived(beside_parts.at[0], beside_sems.at[0])
+    near_extra = beside_parts[0].astype(jnp.float32)
+    owner_send[2] = (chip_sum(2) + jnp.where(odd == 1, near_extra, far_extra)).astype(
+        jnp.bfloat16
+    )
+    send(
+        owner_send.at[2], owner_parts.at[1], owner_sems.at[1], (away(-2), final_lane)
+    )
+    owner_send[0] = (chip_sum(0) + jnp.where(odd == 1, 0.0, near_extra)).astype(jnp.bfloat16)
+    send(
+        owner_send.at[0], owner_parts.at[0], owner_sems.at[0], (place, final_lane), crossing
+    )
+
+    for steps in range(1, pair_count):
+        owner_pair = pair_away(steps)
+        owner = 2 * owner_pair + odd
+        arrived(sum_beside.at[owner_pair], sum_beside_sems.at[owner_pair])
+        sum_send[owner] = (
+            sum_send[owner].astype(jnp.float32) + sum_beside[owner_pair].astype(jnp.float32)
+        ).astype(jnp.bfloat16)
+        send(
+            sum_send.at[owner],
+            sum_parts.at[pair_place],
+            sum_sems.at[pair_place],
+            (owner, lane),
+        )
+    arrived(sum_beside.at[pair_place], sum_beside_sems.at[pair_place])
+    gradient = sum_send[place].astype(jnp.float32) + sum_beside[pair_place].astype(jnp.float32)
+    for steps in range(1, pair_count):
+        source = pair_away(-steps)
         arrived(sum_parts.at[source], sum_sems.at[source])
         gradient = gradient + sum_parts[source].astype(jnp.float32)
     down_gradient = jnp.concatenate(
@@ -639,6 +692,7 @@
     up_gradient = jnp.concatenate(
         [gradient[:local_rows, down_half:], gradient[local_rows:, down_half:]], 1
     )
+    ready(5, 6, 8, 9)
     new_down_ref[...], new_down_one_ref[...], new_down_two_ref[...] = adam_update(
         own_down, down_one_ref[...], down_two_ref[...], down_gradient
     )
@@ -655,7 +709,7 @@
         owner_parts[0] = owner_send[0]
 
     part_sum = owner_parts[0].astype(jnp.float32)
-    for slot in range(1, reach + 1):
+    for slot in range(1, reach // 2 + 1):
         arrived(owner_parts.at[slot], owner_sems.at[slot])
         part_sum = part_sum + owner_parts[slot].astype(jnp.float32)
     kv_grad_ref[...] = part_sum.T
@@ -665,6 +719,46 @@
             copy.wait_send()
         else:
             pl.when(when)(copy.wait_send)
+
+
+def fused_kernel(ctx_count, *refs):
+    operands, results, scratch = refs[:13], refs[13:22], refs[22:]
+    local, local_sems = scratch[-14:-1], scratch[-1]
+    loads = [
+        pltpu.make_async_copy(operand, copy, local_sems.at[index])
+        for index, (operand, copy) in enumerate(zip(operands, local))
+    ]
+    for index in (4, 7, 1, 3, 10, 2, 0, 11, 12, 5, 6, 8, 9):
+        loads[index].start()
+
+    def ready(*indices):
+        for index in indices:
+            loads[index].wait()
+
+    layer_body(ctx_count, ready, *local, *results, *scratch[:-14])
+
+
+def publish_kernel(*refs):
+    count = len(refs) // 2
+    copies = [
+        pltpu.make_async_copy(refs[index], refs[count + index], refs[-1].at[index])
+        for index in range(count)
+    ]
+    for copy in copies:
+        copy.start()
+    for copy in copies:
+        copy.wait()
+
+
+def publish(values):
+    return pl.pallas_call(
+        publish_kernel,
+        out_shape=[jax.ShapeDtypeStruct(value.shape, value.dtype) for value in values],
+        in_specs=[pl.BlockSpec(memory_space=pl.ANY)] * len(values),
+        out_specs=[pl.BlockSpec(memory_space=pltpu.HBM)] * len(values),
+        scratch_shapes=[pltpu.SemaphoreType.DMA((len(values),))],
+        compiler_params=pltpu.CompilerParams(vmem_limit_bytes=VMEM_GRANT),
+    )(*values)
 
 
 def fused(*args):
@@ -679,7 +773,7 @@
     block = (2 * local_rows, (down.shape[1] + up.shape[1]) // 2)
     half_type, full_type = jnp.bfloat16, jnp.float32
     in_vmem = pl.BlockSpec(memory_space=pltpu.VMEM)
-    in_smem = pl.BlockSpec(memory_space=pltpu.SMEM)
+    in_hbm = pl.BlockSpec(memory_space=pltpu.HBM)
     shapes = [
         (frozen.shape, half_type),
         (frozen.shape, half_type),
@@ -694,7 +788,7 @@
     return pl.pallas_call(
         functools.partial(fused_kernel, ctx_count),
         out_shape=[jax.ShapeDtypeStruct(shape, kind) for shape, kind in shapes],
-        in_specs=[in_vmem] * 11 + [in_smem] * 2,
+        in_specs=[in_hbm] * len(args),
         out_specs=[in_vmem] * 9,
         scratch_shapes=[
             pltpu.VMEM((ctx_count,) + block, half_type),
@@ -711,20 +805,27 @@
             pltpu.VMEM((reach + 1, HEAD_SIZE, tokens), half_type),
             pltpu.VMEM((reach + 1, HEAD_SIZE, tokens), half_type),
             pltpu.VMEM((reach + 1, HEAD_SIZE, tokens), half_type),
-            pltpu.VMEM((reach + 1, HEAD_SIZE, tokens), half_type),
+            pltpu.VMEM((reach // 2 + 1, HEAD_SIZE, tokens), half_type),
+            pltpu.VMEM((2, HEAD_SIZE, tokens), half_type),
             pltpu.VMEM((ctx_count,) + block, half_type),
-            pltpu.VMEM((ctx_count,) + block, half_type),
+            pltpu.VMEM((ctx_count // 2,) + block, half_type),
+            pltpu.VMEM((ctx_count // 2,) + block, half_type),
             pltpu.SemaphoreType.DMA((64,)),
             pltpu.SemaphoreType.DMA((ctx_count,)),
             pltpu.SemaphoreType.DMA((reach + 1, 2)),
             pltpu.SemaphoreType.DMA((head_count,)),
             pltpu.SemaphoreType.DMA((head_count,)),
             pltpu.SemaphoreType.DMA((reach + 1,)),
-            pltpu.SemaphoreType.DMA((reach + 1,)),
-            pltpu.SemaphoreType.DMA((ctx_count,)),
-        ],
+            pltpu.SemaphoreType.DMA((reach // 2 + 1,)),
+            pltpu.SemaphoreType.DMA((2,)),
+            pltpu.SemaphoreType.DMA((ctx_count // 2,)),
+            pltpu.SemaphoreType.DMA((ctx_count // 2,)),
+        ]
+        + [pltpu.VMEM(arg.shape, arg.dtype) for arg in args[:11]]
+        + [pltpu.SMEM(arg.shape, arg.dtype) for arg in args[11:]]
+        + [pltpu.SemaphoreType.DMA((len(args),))],
         compiler_params=pltpu.CompilerParams(
-            collective_id=0, has_side_effects=True, vmem_limit_bytes=40 * 1024 * 1024
+            collective_id=0, has_side_effects=True, vmem_limit_bytes=VMEM_GRANT
         ),
     )(*args)
 
@@ -736,7 +837,7 @@
         and args[4].shape[0] % 8 == 0
         and lax.axis_size("head") == 2 * KVH
     )
-    return tuple(fused(*args)) if fits else on_device(*args)
+    return tuple(publish(fused(*args))) if fits else on_device(*args)
 
 
 def solution(mesh):

time: 62.4 us -> 71 us (1.14)
  the two profiles are of different devices: /device:TPU:29 before, /device:TPU:0 now
where the time goes in v2:
time: 71 us; the launch traced here: 70.9 us
  Pallas kernels  70.2 us (99%)
    pallas_call x1, Pallas kernels, fused(): pl.pallas_call(functools.partial(fused_kernel, ctx_count), out_shape=[jax...  41.7 us
    pallas_call x1, Pallas kernels, publish(): pl.pallas_call(publish_kernel, out_shape=[jax.ShapeDtypeStruct(value.shap...  28.5 us

profile of v2, /device:TPU:0, one launch (start us, length us, event | category | flops | bytes accessed | tf_op | source)
XLA Modules:
  0.0 70.9 jit_solution(2709068919914155031)
XLA Ops:
  0.6 41.7 %shard_map.196 = (bf16[256,512]{1,0:T(8,128)(2,1)}, bf16[256,512]{1,0:T(8,128)(2,1)}, f32[256,128]{1,0:T(8,128)}, f32[8,2048]{1,0:T(8,128)}, f32[8,2048]{1,0:T(8...) custom-call(bf16[256,512]{1,0:T(8,128)(2,1)} %refs_0_.1, ...), custom_call_target="tpu_custom_call" | custom-call | tf_op jit(solution)/shard_map/pallas_call | solution.py:788
  42.4 28.5 %shard_map.197 = (bf16[256,512]{1,0:T(8,128)(2,1)}, bf16[256,512]{1,0:T(8,128)(2,1)}, f32[256,128]{1,0:T(8,128)}, f32[8,2048]{1,0:T(8,128)}, f32[8,2048]{1,0:T(8...) custom-call(bf16[256,512]{1,0:T(8,128)(2,1)} %get-tuple-element.18.refs_0_, ...), custom_call_target="tpu_custom_call" | custom-call | tf_op jit(solution)/shard_map/pallas_call | solution.py:754

commit v3 on v2

--- a/solution.py
+++ b/solution.py
@@ -738,25 +738,34 @@
     layer_body(ctx_count, ready, *local, *results, *scratch[:-14])
 
 
-def publish_kernel(*refs):
-    count = len(refs) // 2
-    copies = [
-        pltpu.make_async_copy(refs[index], refs[count + index], refs[-1].at[index])
+def publish_kernel(count, *refs):
+    values, results, staged = refs[:count], refs[count : 2 * count], refs[2 * count : -1]
+    loads = [
+        pltpu.make_async_copy(values[index], staged[index], refs[-1].at[0, index])
         for index in range(count)
     ]
-    for copy in copies:
-        copy.start()
-    for copy in copies:
-        copy.wait()
+    stores = [
+        pltpu.make_async_copy(staged[index], results[index], refs[-1].at[1, index])
+        for index in range(count)
+    ]
+    for load in loads:
+        load.start()
+    for load, store in zip(loads, stores):
+        load.wait()
+        store.start()
+    for store in stores:
+        store.wait()
 
 
 def publish(values):
+    count = len(values)
     return pl.pallas_call(
-        publish_kernel,
+        functools.partial(publish_kernel, count),
         out_shape=[jax.ShapeDtypeStruct(value.shape, value.dtype) for value in values],
-        in_specs=[pl.BlockSpec(memory_space=pl.ANY)] * len(values),
-        out_specs=[pl.BlockSpec(memory_space=pltpu.HBM)] * len(values),
-        scratch_shapes=[pltpu.SemaphoreType.DMA((len(values),))],
+        in_specs=[pl.BlockSpec(memory_space=pltpu.HBM)] * count,
+        out_specs=[pl.BlockSpec(memory_space=pltpu.HBM)] * count,
+        scratch_shapes=[pltpu.VMEM(value.shape, value.dtype) for value in values]
+        + [pltpu.SemaphoreType.DMA((2, count))],
         compiler_params=pltpu.CompilerParams(vmem_limit_bytes=VMEM_GRANT),
     )(*values)
 

time: 71 us -> 44.6 us (0.63)
  Pallas kernels: 70.2 us -> 43.8 us
    pallas_call x1, Pallas kernels: 28.5 us -> 2.01 us  [publish(): pl.pallas_call(functools.partial(publish_kernel, count), out_shape=[jax.S...]
where the time goes in v3:
time: 44.6 us; the launch traced here: 44.4 us
  Pallas kernels  43.8 us (98%)
  between operations  0.66 us (1%)
    pallas_call x1, Pallas kernels, fused(): pl.pallas_call(functools.partial(fused_kernel, ctx_count), out_shape=[jax...  41.7 us
    pallas_call x1, Pallas kernels, publish(): pl.pallas_call(functools.partial(publish_kernel, count), out_shape=[jax.S...  2.01 us

profile of v3, /device:TPU:0, one launch (start us, length us, event | category | flops | bytes accessed | tf_op | source)
XLA Modules:
  0.0 44.4 jit_solution(15735894570414229003)
XLA Ops:
  0.6 41.7 %shard_map.196 = (bf16[256,512]{1,0:T(8,128)(2,1)}, bf16[256,512]{1,0:T(8,128)(2,1)}, f32[256,128]{1,0:T(8,128)}, f32[8,2048]{1,0:T(8,128)}, f32[8,2048]{1,0:T(8...) custom-call(bf16[256,512]{1,0:T(8,128)(2,1)} %refs_0_.1, ...), custom_call_target="tpu_custom_call" | custom-call | tf_op jit(solution)/shard_map/pallas_call | solution.py:797
  42.4 2.0 %shard_map.197 = (bf16[256,512]{1,0:T(8,128)(2,1)}, bf16[256,512]{1,0:T(8,128)(2,1)}, f32[256,128]{1,0:T(8,128)}, f32[8,2048]{1,0:T(8,128)}, f32[8,2048]{1,0:T(8...) custom-call(bf16[256,512]{1,0:T(8,128)(2,1)} %get-tuple-element.18.refs_0_, ...), custom_call_target="tpu_custom_call" | custom-call | tf_op jit(solution)/shard_map/pallas_call | solution.py:762
